TPU v7x, 512 devices: a whole 4x4x16 slice. The times are simulated.
512 devices in a mesh: row: 32 (over y, x, core), col: 16 (over z).
Axes of the slice: x: 4, y: 4, z: 16, core: 2. Of those that a mesh axis runs over, the one named last changes fastest.
Arguments:
- tokens: bfloat16 [4096, 6144], P('row', 'col'), may hold values from -6 to 6
- weight_blocks: bfloat16 [16, 128, 4096], P('col', 'row'), may hold values from -0.375 to 0.375
- block_rows: int32 [16, 128], P('col', 'row'), may hold values from 0 to 95, as said below
- block_columns: int32 [16, 128], P('col', 'row'), may hold values from 0 to 47
- panel_counts: int32 [16], P('col'), may hold values from 16 to 128, as said below
- hidden_grad: bfloat16 [4096, 49152], P('row', 'col'), may hold values from -1.1953125 to 1.1953125
Outputs:
- hidden: bfloat16 [4096, 49152], P('row', 'col')
- input_grad: bfloat16 [4096, 6144], P('row', 'col')
- weight_grad: bfloat16 [16, 128, 4096], P('col', 'row')
Inputs may be any that keep to these rules, and one draw needn't show every extreme that they name: `block_rows`: in each panel the live slots name distinct pairs of block row and block column; ids in the other slots lie in the same ranges and mean nothing. `panel_counts`: some panel has all 128 slots live.
All inputs are finite; a program needn't handle non-finite values.
Results may differ from a plain program's by a relative error of at most 0.02.
Values may be sent and summed in bfloat16 or wider, within the bound.
No kernel may reach another device: no remote copies, remote signals or barrier semaphores. Data moves between devices by JAX's collectives and lax.ppermute only.
A program may use at most 64 MiB of HBM per device.

v0:
```python
import math
import jax
import jax.numpy as jnp
from jax import lax
from jax.sharding import PartitionSpec as P

root_two_pi = 0.7978845608028654
cubic_term = 0.044715


def gelu_value(pre_act):
    inner = root_two_pi * (pre_act + cubic_term * pre_act * pre_act * pre_act)
    return 0.5 * pre_act * (1.0 + jnp.tanh(inner))


def gelu_slope(pre_act):
    inner = root_two_pi * (pre_act + cubic_term * pre_act * pre_act * pre_act)
    tangent = jnp.tanh(inner)
    return 0.5 * (1.0 + tangent) + 0.5 * pre_act * (1.0 - tangent * tangent) * root_two_pi * (
        1.0 + 3.0 * cubic_term * pre_act * pre_act
    )


def grouped_inputs(blocks, rows_here, cols_here, live_here):
    length = rows_here.shape[0]
    stride = max([width for width in range(1, 65) if length % width == 0])
    group_count = length // stride
    block_side = math.isqrt(blocks.shape[-1])
    shaped = blocks.reshape(group_count, stride, block_side, block_side)
    return (
        shaped,
        rows_here.reshape(group_count, stride),
        cols_here.reshape(group_count, stride),
        live_here.reshape(group_count, stride),
    )


def forward_blocks(running_start, token_blocks, blocks, rows_here, cols_here, live_here):
    tok_rows = token_blocks.shape[0]
    block_side = token_blocks.shape[2]

    def forward_advance(running, inputs):
        part_blocks, part_rows, part_cols, part_live = inputs
        masked = jnp.where(part_live[:, None, None], part_blocks, jnp.zeros_like(part_blocks))
        picked = jnp.take(token_blocks, part_rows, axis=1)
        products = jnp.einsum("tsa,sab->stb", picked, masked, preferred_element_type=jnp.float32)
        return (
            running.at[part_cols].add(products.reshape(part_rows.shape[0], tok_rows * block_side)),
            None,
        )

    result, unused = lax.scan(
        forward_advance, running_start, grouped_inputs(blocks, rows_here, cols_here, live_here)
    )
    return result


def backward_blocks(running_start, grad_blocks, blocks, rows_here, cols_here, live_here):
    tok_rows = grad_blocks.shape[0]
    block_side = grad_blocks.shape[2]

    def backward_advance(running, inputs):
        part_blocks, part_rows, part_cols, part_live = inputs
        masked = jnp.where(part_live[:, None, None], part_blocks, jnp.zeros_like(part_blocks))
        picked = jnp.take(grad_blocks, part_cols, axis=1)
        products = jnp.einsum("tsb,sab->sta", picked, masked, preferred_element_type=jnp.float32)
        return (
            running.at[part_rows].add(products.reshape(part_rows.shape[0], tok_rows * block_side)),
            None,
        )

    result, unused = lax.scan(
        backward_advance, running_start, grouped_inputs(blocks, rows_here, cols_here, live_here)
    )
    return result


def on_device(tokens, weight_blocks, block_rows, block_columns, panel_counts, hidden_grad):
    whole = lax.all_gather(tokens, "col", axis=1, tiled=True)
    tok_rows = whole.shape[0]
    block_side = math.isqrt(weight_blocks.shape[2])
    row_blocks = whole.shape[1] // block_side
    col_blocks = hidden_grad.shape[1] // block_side
    per_device = weight_blocks.shape[1]
    capacity = per_device * lax.axis_size("row")
    count_live = panel_counts[0]
    token_blocks = whole.reshape(tok_rows, row_blocks, block_side)
    empty_pre = jnp.zeros((col_blocks, tok_rows * block_side), jnp.float32)
    empty_ids = jnp.zeros((capacity,), jnp.int32)
    shard_piece = (
        lax.all_gather(weight_blocks, "row", axis=1, tiled=True),
        lax.all_gather(block_rows, "row", axis=1, tiled=True),
        lax.all_gather(block_columns, "row", axis=1, tiled=True),
    )
    begin_at = jnp.int32(0)
    pre_sum = empty_pre
    fold_rows_all = empty_ids
    fold_cols_all = empty_ids
    rows_here = shard_piece[1][0]
    cols_here = shard_piece[2][0]
    live_here = jnp.arange(rows_here.shape[0], dtype=jnp.int32) < count_live
    pre_sum = forward_blocks(
        pre_sum, token_blocks, shard_piece[0][0], rows_here, cols_here, live_here
    )
    fold_rows_all = lax.dynamic_update_slice_in_dim(fold_rows_all, rows_here, begin_at, 0)
    fold_cols_all = lax.dynamic_update_slice_in_dim(fold_cols_all, cols_here, begin_at, 0)
    pre_sum, rows_all, cols_all = (pre_sum, fold_rows_all, fold_cols_all)
    pre_act = pre_sum.reshape(col_blocks, tok_rows, block_side).transpose(1, 0, 2)
    hidden = gelu_value(pre_act).astype(jnp.bfloat16).reshape(tok_rows, col_blocks * block_side)
    upstream = hidden_grad.reshape(tok_rows, col_blocks, block_side)
    grad_blocks = (upstream.astype(jnp.float32) * gelu_slope(pre_act)).astype(jnp.bfloat16)
    empty_back = jnp.zeros((row_blocks, tok_rows * block_side), jnp.float32)
    shard_piece = (
        lax.all_gather(weight_blocks, "row", axis=1, tiled=True),
        lax.all_gather(block_rows, "row", axis=1, tiled=True),
        lax.all_gather(block_columns, "row", axis=1, tiled=True),
    )
    rows_here = shard_piece[1][0]
    cols_here = shard_piece[2][0]
    live_here = jnp.arange(rows_here.shape[0], dtype=jnp.int32) < count_live
    input_part = backward_blocks(
        empty_back, grad_blocks, shard_piece[0][0], rows_here, cols_here, live_here
    )
    own_sums = lax.psum_scatter(
        input_part.astype(jnp.bfloat16), "col", scatter_dimension=0, tiled=True
    ).astype(jnp.float32)
    input_grad = (
        own_sums.reshape(-1, tok_rows, block_side)
        .transpose(1, 0, 2)
        .reshape(tok_rows, -1)
        .astype(jnp.bfloat16)
    )
    live_part = jnp.arange(per_device * lax.axis_size("row"), dtype=jnp.int32) < count_live
    picked_in = jnp.take(token_blocks, rows_all, axis=1)
    picked_grad = jnp.take(grad_blocks, cols_all, axis=1)
    products = jnp.einsum(
        "tsa,tsb->sab", picked_in, picked_grad, preferred_element_type=jnp.float32
    )
    products = jnp.where(live_part[:, None, None], products, jnp.zeros_like(products))
    weight_sum = lax.psum_scatter(
        products.reshape(per_device * lax.axis_size("row"), block_side * block_side).astype(
            jnp.bfloat16
        ),
        "row",
        scatter_dimension=0,
        tiled=True,
    )
    weight_grad = weight_sum.reshape(1, per_device, block_side * block_side)
    return (hidden, input_grad, weight_grad)


def solution(mesh):
    placed = (
        P("row", "col"),
        P("col", "row", None),
        P("col", "row"),
        P("col", "row"),
        P("col"),
        P("row", "col"),
    )
    return jax.shard_map(
        on_device,
        mesh=mesh,
        in_specs=placed,
        out_specs=(P("row", "col"), P("row", "col"), P("col", "row", None)),
        check_vma=False,
    )
```

profile of v0, /device:TPU:1, one launch (start us, length us, event | category | flops | bytes accessed | tf_op | source)
XLA Modules:
  0.0 446.8 jit_solution(2087213582369064578)
XLA Ops:
  15.8 14.4 %all-reduce.5 = (s32[128]{0:T(128)S(1)}, s32[128]{0:T(128)S(1)}) all-reduce(s32[128]{0:T(128)S(1)} %bitcast_dynamic-update-slice_fusion.1, s32[128]{0:T(128)S(1)} %bitcast_dynamic-update-slice_fusion), channel_id=1, replica_groups=mesh['row'=32,'col'=16] {'row'}, use_global_device_ids=true, to_apply=%add | all-reduce | flops 256 | bytes 2048 | tf_op jit(solution)/shard_map/squeeze | solution.py:100
  35.5 41.1 %all-gather.5.cloned.1.call-done = bf16[1,128,4096]{2,0,1:T(2,128)(2,1)} async-done(((bf16[1,4,4096]{2,0,1:T(2,128)(2,1)}), bf16[1,128,4096]{2,0,1:T(2,128)(2,1)}) %all-gather.5.cloned.1.call-update) | async-done | bytes 1048592 | tf_op jit(solution)/shard_map/all_gather | solution.py:91
  76.6 7.7 %reduce = bf16[128,4096]{1,0:T(8,128)(2,1)S(1)} reduce(bf16[1,128,4096]{2,0,1:T(2,128)(2,1)} %all-gather.5.cloned.1.call-done, bf16[]{:T(256)} %constant.132), dimensions={0}, to_apply=%all_gather.18.reduce_sub_computation | reduce | bytes 2097154 | tf_op jit(solution)/shard_map/all_gather | solution.py:91
  87.8 53.0 %all-gather.3.cloned.1.call-done = bf16[128,6144]{0,1:T(8,128)(2,1)} async-done(((bf16[128,384]{0,1:T(8,128)(2,1)}), bf16[128,6144]{0,1:T(8,128)(2,1)}) %all-gather.3.cloned.1.call-update) | async-done | bytes 1572880 | tf_op jit(solution)/shard_map/all_gather | solution.py:79
  140.9 40.8 %while.20 = (s32[]{:T(128)}, f32[48,8192]{1,0:T(8,128)S(1)}, s32[2,64]{1,0:T(2,128)S(1)}, s32[2,64]{1,0:T(2,128)S(1)}, bf16[128,96,64]{0,2,1:T(8,128)(2,1)}, /*i...) while((s32[]{:T(128)}, f32[48,8192]{1,0:T(8,128)S(1)}, s32[2,64]{1,0:T(2,128)S(1)}, ...), condition=%wide.region_2.3_spmd, body=%wide.region_0.2_spmd.sunk | while | flops 68421376 | bytes 18356652 | solution.py:52
  147.8 4.1 fusion.54
  151.9 4.8 %reshape.324 = f32[64,8192]{1,0:T(8,128)} reshape(f32[64,128,64]{2,1,0:T(8,128)} %fusion.54) | data formatting | bytes 4194304 | tf_op jit(solution)/shard_map/while/body/eval_jaxpr/reshape | solution.py:48
  156.7 4.6 %scatter_fusion = f32[48,8192]{1,0:T(8,128)S(1)} fusion(f32[48,8192]{1,0:T(8,128)S(1)} %get-tuple-element.269, s32[64]{0:T(128)S(1)} %get-tuple-element.249, f32[64,8192]{1,0:T(8,128)} %reshape.324), kind=kCustom, calls=%fused_computation.4.clone.1 | custom fusion | flops 524288 | bytes 6291712 | tf_op jit(solution)/shard_map/while/body/eval_jaxpr/scatter-add | solution.py:48
  168.1 4.1 fusion.54
  172.2 4.8 %reshape.324 = f32[64,8192]{1,0:T(8,128)} reshape(f32[64,128,64]{2,1,0:T(8,128)} %fusion.54) | data formatting | bytes 4194304 | tf_op jit(solution)/shard_map/while/body/eval_jaxpr/reshape | solution.py:48
  177.1 4.6 %scatter_fusion = f32[48,8192]{1,0:T(8,128)S(1)} fusion(f32[48,8192]{1,0:T(8,128)S(1)} %get-tuple-element.269, s32[64]{0:T(128)S(1)} %get-tuple-element.249, f32[64,8192]{1,0:T(8,128)} %reshape.324), kind=kCustom, calls=%fused_computation.4.clone.1 | custom fusion | flops 524288 | bytes 6291712 | tf_op jit(solution)/shard_map/while/body/eval_jaxpr/scatter-add | solution.py:48
  189.1 34.9 %while.21 = (s32[]{:T(128)}, f32[96,8192]{1,0:T(8,128)S(1)}, s32[2,64]{1,0:T(2,128)S(1)}, s32[2,64]{1,0:T(2,128)S(1)}, bf16[128,48,64]{0,2,1:T(8,128)(2,1)}, /*i...) while((s32[]{:T(128)}, f32[96,8192]{1,0:T(8,128)S(1)}, s32[2,64]{1,0:T(2,128)S(1)}, ...), condition=%wide.region_5.6_spmd, body=%wide.region_3.5_spmd.sunk | while | flops 68421376 | bytes 16783788 | solution.py:72
  192.2 4.4 fusion.57
  196.6 4.8 %reshape.329 = f32[64,8192]{1,0:T(8,128)} reshape(f32[64,128,64]{2,1,0:T(8,128)} %fusion.57) | data formatting | bytes 4194304 | tf_op jit(solution)/shard_map/while/body/eval_jaxpr/reshape | solution.py:68
  201.4 5.2 %scatter_fusion.1 = f32[96,8192]{1,0:T(8,128)S(1)} fusion(f32[96,8192]{1,0:T(8,128)S(1)} %get-tuple-element.293, s32[64]{0:T(128)S(1)} %get-tuple-element.258, f32[64,8192]{1,0:T(8,128)} %reshape.329), kind=kCustom, calls=%fused_computation.5.clone.1 | custom fusion | flops 524288 | bytes 6291712 | tf_op jit(solution)/shard_map/while/body/eval_jaxpr/scatter-add | solution.py:68
  209.5 4.4 fusion.57
  213.9 4.8 %reshape.329 = f32[64,8192]{1,0:T(8,128)} reshape(f32[64,128,64]{2,1,0:T(8,128)} %fusion.57) | data formatting | bytes 4194304 | tf_op jit(solution)/shard_map/while/body/eval_jaxpr/reshape | solution.py:68
  218.7 5.2 %scatter_fusion.1 = f32[96,8192]{1,0:T(8,128)S(1)} fusion(f32[96,8192]{1,0:T(8,128)S(1)} %get-tuple-element.293, s32[64]{0:T(128)S(1)} %get-tuple-element.258, f32[64,8192]{1,0:T(8,128)} %reshape.329), kind=kCustom, calls=%fused_computation.5.clone.1 | custom fusion | flops 524288 | bytes 6291712 | tf_op jit(solution)/shard_map/while/body/eval_jaxpr/scatter-add | solution.py:68
  225.3 33.0 %fusion = bf16[8,8192]{1,0:T(8,128)(2,1)S(1)} fusion(bf16[96,8192]{1,0:T(8,128)(2,1)} %convert_element_type.36), kind=kCustom, calls=%all-reduce-scatter | all-reduce-scatter fusion | flops 1048577 | bytes 1705984
  258.3 3.7 collective-permute-start.2
  261.9 4.3 collective-permute-start.1
  272.4 4.8 %fusion.27 = bf16[128,64,64]{2,1,0:T(8,128)(2,1)} fusion(bf16[128,128,64]{1,2,0:T(8,128)(2,1)} %gather_fusion.3, bf16[128,128,64]{1,2,0:T(8,128)(2,1)} %gather_fusion.2, pred[128]{0:T(512)(128)(4,1)S(1)} %copy-done.4, pred[128]{0:T(512)(128)(4,1)S(1)} %copy-done.5), kind=kOutput, calls=%fused_computation.53 | convolution fusion | flops 136314880 | bytes 5243136 | tf_op jit(solution)/shard_map/tsa,tsb->sab/dot_general | solution.py:136
  280.6 5.1 %collective-permute-start.3 = (bf16[6,8192]{1,0:T(8,128)(2,1)S(1)}, bf16[6,8192]{1,0:T(8,128)(2,1)S(1)}, u32[]{:S(2)}, u32[]{:S(2)}) collective-permute-start(bf16[6,8192]{1,0:T(8,128)(2,1)S(1)} %slice.8), channel_id=1, source_target_pairs={{0,4},{1,5},{2,6},{3,7},{4,8},{5,9},{6,10},{7,11},{8,12},{9,13},{1... | collective-permute-start | bytes 294920
  291.2 146.5 %all-reduce.8.cloned.1.call-done = bf16[128,4096]{0,1:T(8,128)(2,1)} async-done(((bf16[128,4096]{0,1:T(8,128)(2,1)}), bf16[128,4096]{0,1:T(8,128)(2,1)}) %all-reduce.8.cloned.1.call-update) | async-done | bytes 1048592
  (85 shorter events, 60.4 us)
Async XLA Ops:
  7.2 69.4 %all-gather.5.cloned.1.call-start = ((), (), s32[]{:S(2)}) async-start(), calls=%async_computation.1 | async-start | bytes 2162688 | tf_op jit(solution)/shard_map/all_gather | solution.py:91
  8.7 132.1 %all-gather.3.cloned.1.call-start = ((), (), s32[]{:S(2)}) async-start(), calls=%async_computation | async-start | bytes 1671168 | tf_op jit(solution)/shard_map/all_gather | solution.py:79
  10.4 427.3 %all-reduce.8.cloned.1.call-start = ((), (), s32[]{:S(2)}) async-start(), calls=%async_computation.2 | async-start | bytes 2097152
  225.3 42.3 %copy-start = (bf16[128,48,64]{0,2,1:T(8,128)(2,1)S(1)}, bf16[128,48,64]{0,2,1:T(8,128)(2,1)}, u32[]{:S(2)}) copy-start(bf16[128,48,64]{0,2,1:T(8,128)(2,1)} %get-tuple-element.311) | copy-start | bytes 2359300
  258.3 30.2 %collective-permute-start.2 = (bf16[8,8192]{1,0:T(8,128)(2,1)S(1)}, bf16[8,8192]{1,0:T(8,128)(2,1)S(1)}, u32[]{:S(2)}, u32[]{:S(2)}) collective-permute-start(bf16[8,8192]{1,0:T(8,128)(2,1)S(1)} %fusion), channel_id=1, source_target_pairs={{0,3},{1,4},{2,5},{3,6},{4,7},{5,8},{6,9},{7,10},{8,11},{9,12},{10... | collective-permute-start | bytes 393224
  261.9 26.6 %collective-permute-start.1 = (bf16[8,8192]{1,0:T(8,128)(2,1)S(1)}, bf16[8,8192]{1,0:T(8,128)(2,1)S(1)}, u32[]{:S(2)}, u32[]{:S(2)}) collective-permute-start(bf16[8,8192]{1,0:T(8,128)(2,1)S(1)} %fusion), channel_id=1, source_target_pairs={{0,2},{1,3},{2,4},{3,5},{4,6},{5,7},{6,8},{7,9},{8,10},{9,11},{10,... | collective-permute-start | bytes 393224
  266.2 22.2 %collective-permute-start = (bf16[8,8192]{1,0:T(8,128)(2,1)S(1)}, bf16[8,8192]{1,0:T(8,128)(2,1)S(1)}, u32[]{:S(2)}, u32[]{:S(2)}) collective-permute-start(bf16[8,8192]{1,0:T(8,128)(2,1)S(1)} %fusion), channel_id=1, source_target_pairs={{0,1},{1,2},{2,3},{3,4},{4,5},{5,6},{6,7},{7,8},{8,9},{9,10},{10,1... | collective-permute-start | bytes 393224
  267.5 2.4 copy-start.1
  270.0 2.4 copy-start.4
  270.0 2.4 copy-start.5
  277.2 8.5 %copy-start.3 = (pred[128]{0:T(512)(128)(4,1)S(1)}, pred[128]{0:T(512)(128)(4,1)}, u32[]{:S(2)}) copy-start(pred[128]{0:T(512)(128)(4,1)} %iota_compare_fusion) | copy-start | bytes 388
  277.2 9.8 %copy-start.2 = (bf16[128,48,64]{0,2,1:T(8,128)(2,1)S(1)}, bf16[128,48,64]{0,2,1:T(8,128)(2,1)}, u32[]{:S(2)}) copy-start(bf16[128,48,64]{0,2,1:T(8,128)(2,1)} %get-tuple-element.161) | copy-start | bytes 2359300
  280.6 7.9 %collective-permute-start.3 = (bf16[6,8192]{1,0:T(8,128)(2,1)S(1)}, bf16[6,8192]{1,0:T(8,128)(2,1)S(1)}, u32[]{:S(2)}, u32[]{:S(2)}) collective-permute-start(bf16[6,8192]{1,0:T(8,128)(2,1)S(1)} %slice.8), channel_id=1, source_target_pairs={{0,4},{1,5},{2,6},{3,7},{4,8},{5,9},{6,10},{7,11},{8,12},{9,13},{1... | collective-permute-start | bytes 294920
Sparse Core Ops, SparseCore 0:
  11.7 64.8 all-gather.4
  79.3 61.5 all-gather.2
  288.3 149.3 all-reduce.7
where the time goes:
time: 448 us; the launch traced here: 447 us
  waiting for transfers between devices  241 us (54%)
  local copies, waits for them, and re-layouts  70.5 us (16%)
  blocking collectives  47.4 us (11%)
  other arithmetic  34.7 us (8%)
  matrix products  21.9 us (5%)
  between operations  16.4 us (4%)
  starting transfers between devices  14.4 us (3%)
    unnamed x8, waiting for transfers between devices  147 us
    all_gather x1, waiting for transfers between devices, on_device(): whole = lax.all_gather(tokens, 'col', axis=1, tiled=True)  53 us
    all_gather x1, waiting for transfers between devices, on_device(): lax.all_gather(weight_blocks, 'row', axis=1, tiled=True)  41.1 us
    unnamed x1, blocking collectives  33 us
    squeeze x1, blocking collectives, on_device(): cols_here = shard_piece[2][0]  14.4 us
    unnamed x5, starting transfers between devices  14.4 us
    unnamed x27, local copies, waits for them, and re-layouts  13.3 us
    scatter-add x2, other arithmetic, backward_advance(): running.at[part_rows]  10.4 us
  transfers between devices with their start and end apart: 7, of which 4 were waited for; matrix products, arithmetic and copies ran while one was open for 9% of the time, Pallas kernels for 0%

commit v1 on v0

--- a/solution.py
+++ b/solution.py
@@ -6,6 +6,27 @@
 
 root_two_pi = 0.7978845608028654
 cubic_term = 0.044715
+
+
+def ring_gather(x, axis, dim):
+    devices, place, extent = (lax.axis_size(axis), lax.axis_index(axis), x.shape[dim])
+    forward = [(i, (i + 1) % devices) for i in range(devices)]
+    left = [(i, (i - 1) % devices) for i in range(devices)]
+    filled = jnp.zeros((*x.shape[:dim], devices * extent, *x.shape[dim + 1 :]), x.dtype)
+    filled = lax.dynamic_update_slice_in_dim(filled, x, place * extent, axis=dim)
+    from_left = from_right = x
+    halfway = devices // 2
+    for hop in range(1, halfway + 1):
+        from_left = lax.ppermute(from_left, axis, forward)
+        filled = lax.dynamic_update_slice_in_dim(
+            filled, from_left, (place - hop) % devices * extent, axis=dim
+        )
+        if hop < devices - halfway:
+            from_right = lax.ppermute(from_right, axis, left)
+            filled = lax.dynamic_update_slice_in_dim(
+                filled, from_right, (place + hop) % devices * extent, axis=dim
+            )
+    return filled
 
 
 def gelu_value(pre_act):
@@ -76,7 +97,7 @@
 
 
 def on_device(tokens, weight_blocks, block_rows, block_columns, panel_counts, hidden_grad):
-    whole = lax.all_gather(tokens, "col", axis=1, tiled=True)
+    whole = ring_gather(tokens, "col", 1)
     tok_rows = whole.shape[0]
     block_side = math.isqrt(weight_blocks.shape[2])
     row_blocks = whole.shape[1] // block_side

time: 448 us -> 417 us (0.931)
  waiting for transfers between devices: 241 us -> 155 us
  starting transfers between devices: 14.4 us -> 69.6 us
    ppermute x0 -> x15, starting transfers between devices: none -> 56.3 us  [the longest x7 41 us: ring_gather(): from_right = lax.ppermute(from_right, axis, left)]
    all_gather x1 -> x0, waiting for transfers between devices: 53 us -> none  [on_device(): whole = lax.all_gather(tokens, 'col', axis=1, tiled=True)]
    all_gather x1, waiting for transfers between devices: 41.1 us -> 0.01 us  [on_device(): lax.all_gather(weight_blocks, 'row', axis=1, tiled=True)]
    ppermute x0 -> x15, waiting for transfers between devices: none -> 9.78 us  [the longest x8 9.55 us: ring_gather(): from_left = lax.ppermute(from_left, axis, forward)]
    unnamed x8 -> x7, waiting for transfers between devices: 147 us -> 145 us
    unnamed x27 -> x29, local copies, waits for them, and re-layouts: 13.3 us -> 12.8 us
  transfers between devices with their start and end apart: 7 -> 21, of which waited for: 4 -> 5; matrix products, arithmetic and copies ran while one was open for 9% -> 6% of each run, Pallas kernels for 0% -> 0%
where the time goes in v1:
time: 417 us; the launch traced here: 415 us
  waiting for transfers between devices  155 us (37%)
  local copies, waits for them, and re-layouts  70.3 us (17%)
  starting transfers between devices  69.6 us (17%)
  blocking collectives  47.6 us (11%)
  other arithmetic  34.1 us (8%)
  matrix products  21.2 us (5%)
  between operations  17.5 us (4%)
    unnamed x7, waiting for transfers between devices  145 us
    ppermute x7, starting transfers between devices, ring_gather(): from_right = lax.ppermute(from_right, axis, left)  41 us
    unnamed x1, blocking collectives  33.7 us
    ppermute x8, starting transfers between devices, ring_gather(): from_left = lax.ppermute(from_left, axis, forward)  15.3 us
    squeeze x1, blocking collectives, on_device(): cols_here = shard_piece[2][0]  13.9 us
    unnamed x5, starting transfers between devices  13.2 us
    unnamed x29, local copies, waits for them, and re-layouts  12.8 us
    scatter-add x2, other arithmetic, backward_advance(): running.at[part_rows]  10.4 us
  transfers between devices with their start and end apart: 21, of which 5 were waited for; matrix products, arithmetic and copies ran while one was open for 6% of the time, Pallas kernels for 0%

profile of v1, /device:TPU:1, one launch (start us, length us, event | category | flops | bytes accessed | tf_op | source)
XLA Modules:
  0.0 415.3 jit_solution(16231112744114037665)
XLA Ops:
  8.2 12.0 %collective-permute-start.1 = (bf16[128,384]{0,1:T(8,128)(2,1)S(1)}, bf16[128,384]{0,1:T(8,128)(2,1)S(1)}, u32[]{:S(2)}, u32[]{:S(2)}) collective-permute-start(bf16[128,384]{0,1:T(8,128)(2,1)S(1)} %copy.58), channel_id=1, source_target_pairs={{0,15},{1,0},{2,1},{3,2},{4,3},{5,4},{6,5},{7,6},{8,7},{9,8},{10,9... | collective-permute-start | bytes 294920 | tf_op jit(solution)/shard_map/ppermute | solution.py:25
  27.2 13.9 %all-reduce.5 = (s32[128]{0:T(128)S(1)}, s32[128]{0:T(128)S(1)}) all-reduce(s32[128]{0:T(128)S(1)} %bitcast_dynamic-update-slice_fusion.1, s32[128]{0:T(128)S(1)} %bitcast_dynamic-update-slice_fusion), channel_id=1, replica_groups=mesh['row'=32,'col'=16] {'row'}, use_global_device_ids=true, to_apply=%add | all-reduce | flops 256 | bytes 2048 | tf_op jit(solution)/shard_map/squeeze | solution.py:121
  48.3 4.8 %collective-permute-start.3 = (bf16[128,384]{0,1:T(8,128)(2,1)S(1)}, bf16[128,384]{0,1:T(8,128)(2,1)S(1)}, u32[]{:S(2)}, u32[]{:S(2)}) collective-permute-start(bf16[128,384]{0,1:T(8,128)(2,1)S(1)} %collective-permute-done.1), channel_id=1, source_target_pairs={{0,15},{1,0},{2,1},{3,2},{4,3},{5,4},{6,5},{7,6},{8,7},{9,8},{10,9... | collective-permute-start | bytes 294920 | tf_op jit(solution)/shard_map/ppermute | solution.py:25
  55.1 4.6 %collective-permute-start.5 = (bf16[128,384]{0,1:T(8,128)(2,1)S(1)}, bf16[128,384]{0,1:T(8,128)(2,1)S(1)}, u32[]{:S(2)}, u32[]{:S(2)}) collective-permute-start(bf16[128,384]{0,1:T(8,128)(2,1)S(1)} %collective-permute-done.3), channel_id=1, source_target_pairs={{0,15},{1,0},{2,1},{3,2},{4,3},{5,4},{6,5},{7,6},{8,7},{9,8},{10,9... | collective-permute-start | bytes 294920 | tf_op jit(solution)/shard_map/ppermute | solution.py:25
  61.7 4.6 %collective-permute-start.7 = (bf16[128,384]{0,1:T(8,128)(2,1)S(1)}, bf16[128,384]{0,1:T(8,128)(2,1)S(1)}, u32[]{:S(2)}, u32[]{:S(2)}) collective-permute-start(bf16[128,384]{0,1:T(8,128)(2,1)S(1)} %collective-permute-done.5), channel_id=1, source_target_pairs={{0,15},{1,0},{2,1},{3,2},{4,3},{5,4},{6,5},{7,6},{8,7},{9,8},{10,9... | collective-permute-start | bytes 294920 | tf_op jit(solution)/shard_map/ppermute | solution.py:25
  68.3 4.6 %collective-permute-start.9 = (bf16[128,384]{0,1:T(8,128)(2,1)S(1)}, bf16[128,384]{0,1:T(8,128)(2,1)S(1)}, u32[]{:S(2)}, u32[]{:S(2)}) collective-permute-start(bf16[128,384]{0,1:T(8,128)(2,1)S(1)} %collective-permute-done.7), channel_id=1, source_target_pairs={{0,15},{1,0},{2,1},{3,2},{4,3},{5,4},{6,5},{7,6},{8,7},{9,8},{10,9... | collective-permute-start | bytes 294920 | tf_op jit(solution)/shard_map/ppermute | solution.py:25
  75.4 5.4 %collective-permute-start.11 = (bf16[128,384]{0,1:T(8,128)(2,1)S(1)}, bf16[128,384]{0,1:T(8,128)(2,1)S(1)}, u32[]{:S(2)}, u32[]{:S(2)}) collective-permute-start(bf16[128,384]{0,1:T(8,128)(2,1)S(1)} %collective-permute-done.9), channel_id=1, source_target_pairs={{0,15},{1,0},{2,1},{3,2},{4,3},{5,4},{6,5},{7,6},{8,7},{9,8},{10,9... | collective-permute-start | bytes 294920 | tf_op jit(solution)/shard_map/ppermute | solution.py:25
  82.8 5.1 %collective-permute-start.13 = (bf16[128,384]{0,1:T(8,128)(2,1)S(1)}, bf16[128,384]{0,1:T(8,128)(2,1)S(1)}, u32[]{:S(2)}, u32[]{:S(2)}) collective-permute-start(bf16[128,384]{0,1:T(8,128)(2,1)S(1)} %collective-permute-done.11), channel_id=1, source_target_pairs={{0,15},{1,0},{2,1},{3,2},{4,3},{5,4},{6,5},{7,6},{8,7},{9,8},{10,9... | collective-permute-start | bytes 294920 | tf_op jit(solution)/shard_map/ppermute | solution.py:25
  89.9 4.6 %collective-permute-done.12 = bf16[128,384]{0,1:T(8,128)(2,1)S(1)} collective-permute-done((bf16[128,384]{0,1:T(8,128)(2,1)S(1)}, bf16[128,384]{0,1:T(8,128)(2,1)S(1)}, u32[]{:S(2)}, u32[]{:S(2)}) %collective-permute-start.12) | collective-permute-done | bytes 98336 | tf_op jit(solution)/shard_map/ppermute | solution.py:20
  96.5 4.6 %collective-permute-done.14 = bf16[128,384]{0,1:T(8,128)(2,1)S(1)} collective-permute-done((bf16[128,384]{0,1:T(8,128)(2,1)S(1)}, bf16[128,384]{0,1:T(8,128)(2,1)S(1)}, u32[]{:S(2)}, u32[]{:S(2)}) %collective-permute-start.14) | collective-permute-done | bytes 98336 | tf_op jit(solution)/shard_map/ppermute | solution.py:20
  103.3 7.7 %reduce = bf16[128,4096]{1,0:T(8,128)(2,1)S(1)} reduce(bf16[1,128,4096]{2,0,1:T(2,128)(2,1)} %all-gather.2.cloned.1.call-done, bf16[]{:T(256)} %constant.241), dimensions={0}, to_apply=%all_gather.14.reduce_sub_computation | reduce | bytes 2097154 | tf_op jit(solution)/shard_map/all_gather | solution.py:112
  114.6 40.8 %while.20 = (s32[]{:T(128)}, f32[48,8192]{1,0:T(8,128)S(1)}, s32[2,64]{1,0:T(2,128)S(1)}, s32[2,64]{1,0:T(2,128)S(1)}, bf16[128,96,64]{0,2,1:T(8,128)(2,1)}, /*i...) while((s32[]{:T(128)}, f32[48,8192]{1,0:T(8,128)S(1)}, s32[2,64]{1,0:T(2,128)S(1)}, ...), condition=%wide.region_2.3_spmd, body=%wide.region_0.2_spmd.sunk | while | flops 68421376 | bytes 18356652 | solution.py:73
  125.6 4.8 %reshape.324 = f32[64,8192]{1,0:T(8,128)} reshape(f32[64,128,64]{2,1,0:T(8,128)} %fusion.54) | data formatting | bytes 4194304 | tf_op jit(solution)/shard_map/while/body/eval_jaxpr/reshape | solution.py:69
  130.4 4.6 %scatter_fusion = f32[48,8192]{1,0:T(8,128)S(1)} fusion(f32[48,8192]{1,0:T(8,128)S(1)} %get-tuple-element.269, s32[64]{0:T(128)S(1)} %get-tuple-element.249, f32[64,8192]{1,0:T(8,128)} %reshape.324), kind=kCustom, calls=%fused_computation.4.clone.1 | custom fusion | flops 524288 | bytes 6291712 | tf_op jit(solution)/shard_map/while/body/eval_jaxpr/scatter-add | solution.py:69
  146.0 4.8 %reshape.324 = f32[64,8192]{1,0:T(8,128)} reshape(f32[64,128,64]{2,1,0:T(8,128)} %fusion.54) | data formatting | bytes 4194304 | tf_op jit(solution)/shard_map/while/body/eval_jaxpr/reshape | solution.py:69
  150.8 4.6 %scatter_fusion = f32[48,8192]{1,0:T(8,128)S(1)} fusion(f32[48,8192]{1,0:T(8,128)S(1)} %get-tuple-element.269, s32[64]{0:T(128)S(1)} %get-tuple-element.249, f32[64,8192]{1,0:T(8,128)} %reshape.324), kind=kCustom, calls=%fused_computation.4.clone.1 | custom fusion | flops 524288 | bytes 6291712 | tf_op jit(solution)/shard_map/while/body/eval_jaxpr/scatter-add | solution.py:69
  162.8 35.0 %while.21 = (s32[]{:T(128)}, f32[96,8192]{1,0:T(8,128)S(1)}, s32[2,64]{1,0:T(2,128)S(1)}, s32[2,64]{1,0:T(2,128)S(1)}, bf16[128,48,64]{0,2,1:T(8,128)(2,1)}, /*i...) while((s32[]{:T(128)}, f32[96,8192]{1,0:T(8,128)S(1)}, s32[2,64]{1,0:T(2,128)S(1)}, ...), condition=%wide.region_5.6_spmd, body=%wide.region_3.5_spmd.sunk | while | flops 68421376 | bytes 16783788 | solution.py:93
  170.4 4.8 %reshape.329 = f32[64,8192]{1,0:T(8,128)} reshape(f32[64,128,64]{2,1,0:T(8,128)} %fusion.57) | data formatting | bytes 4194304 | tf_op jit(solution)/shard_map/while/body/eval_jaxpr/reshape | solution.py:89
  175.2 5.2 %scatter_fusion.1 = f32[96,8192]{1,0:T(8,128)S(1)} fusion(f32[96,8192]{1,0:T(8,128)S(1)} %get-tuple-element.293, s32[64]{0:T(128)S(1)} %get-tuple-element.258, f32[64,8192]{1,0:T(8,128)} %reshape.329), kind=kCustom, calls=%fused_computation.5.clone.1 | custom fusion | flops 524288 | bytes 6291712 | tf_op jit(solution)/shard_map/while/body/eval_jaxpr/scatter-add | solution.py:89
  187.7 4.8 %reshape.329 = f32[64,8192]{1,0:T(8,128)} reshape(f32[64,128,64]{2,1,0:T(8,128)} %fusion.57) | data formatting | bytes 4194304 | tf_op jit(solution)/shard_map/while/body/eval_jaxpr/reshape | solution.py:89
  192.5 5.2 %scatter_fusion.1 = f32[96,8192]{1,0:T(8,128)S(1)} fusion(f32[96,8192]{1,0:T(8,128)S(1)} %get-tuple-element.293, s32[64]{0:T(128)S(1)} %get-tuple-element.258, f32[64,8192]{1,0:T(8,128)} %reshape.329), kind=kCustom, calls=%fused_computation.5.clone.1 | custom fusion | flops 524288 | bytes 6291712 | tf_op jit(solution)/shard_map/while/body/eval_jaxpr/scatter-add | solution.py:89
  199.1 33.7 %fusion = bf16[8,8192]{1,0:T(8,128)(2,1)S(1)} fusion(bf16[96,8192]{1,0:T(8,128)(2,1)} %convert_element_type.36), kind=kCustom, calls=%all-reduce-scatter | all-reduce-scatter fusion | flops 1048577 | bytes 1705984
  249.1 6.8 %collective-permute-start.18 = (bf16[6,8192]{1,0:T(8,128)(2,1)S(1)}, bf16[6,8192]{1,0:T(8,128)(2,1)S(1)}, u32[]{:S(2)}, u32[]{:S(2)}) collective-permute-start(bf16[6,8192]{1,0:T(8,128)(2,1)S(1)} %slice.8), channel_id=1, source_target_pairs={{0,4},{1,5},{2,6},{3,7},{4,8},{5,9},{6,10},{7,11},{8,12},{9,13},{1... | collective-permute-start | bytes 294920
  261.1 144.8 %all-reduce.8.cloned.1.call-done = bf16[128,4096]{0,1:T(8,128)(2,1)} async-done(((bf16[128,4096]{0,1:T(8,128)(2,1)}), bf16[128,4096]{0,1:T(8,128)(2,1)}) %all-reduce.8.cloned.1.call-update) | async-done | bytes 1048592
  (131 shorter events, 101.5 us)
Async XLA Ops:
  7.2 96.1 %all-gather.2.cloned.1.call-start = ((), (), s32[]{:S(2)}) async-start(), calls=%async_computation | async-start | bytes 2162688 | tf_op jit(solution)/shard_map/all_gather | solution.py:112
  8.2 40.0 %collective-permute-start.1 = (bf16[128,384]{0,1:T(8,128)(2,1)S(1)}, bf16[128,384]{0,1:T(8,128)(2,1)S(1)}, u32[]{:S(2)}, u32[]{:S(2)}) collective-permute-start(bf16[128,384]{0,1:T(8,128)(2,1)S(1)} %copy.58), channel_id=1, source_target_pairs={{0,15},{1,0},{2,1},{3,2},{4,3},{5,4},{6,5},{7,6},{8,7},{9,8},{10,9... | collective-permute-start | bytes 294920 | tf_op jit(solution)/shard_map/ppermute | solution.py:25
  20.2 32.9 %collective-permute-start = (bf16[128,384]{0,1:T(8,128)(2,1)S(1)}, bf16[128,384]{0,1:T(8,128)(2,1)S(1)}, u32[]{:S(2)}, u32[]{:S(2)}) collective-permute-start(bf16[128,384]{0,1:T(8,128)(2,1)S(1)} %copy.58), channel_id=1, source_target_pairs={{0,1},{1,2},{2,3},{3,4},{4,5},{5,6},{6,7},{7,8},{8,9},{9,10},{10,1... | collective-permute-start | bytes 294920 | tf_op jit(solution)/shard_map/ppermute | solution.py:20
  23.6 382.3 %all-reduce.8.cloned.1.call-start = ((), (), s32[]{:S(2)}) async-start(), calls=%async_computation.1 | async-start | bytes 2097152
  48.3 6.8 %collective-permute-start.3 = (bf16[128,384]{0,1:T(8,128)(2,1)S(1)}, bf16[128,384]{0,1:T(8,128)(2,1)S(1)}, u32[]{:S(2)}, u32[]{:S(2)}) collective-permute-start(bf16[128,384]{0,1:T(8,128)(2,1)S(1)} %collective-permute-done.1), channel_id=1, source_target_pairs={{0,15},{1,0},{2,1},{3,2},{4,3},{5,4},{6,5},{7,6},{8,7},{9,8},{10,9... | collective-permute-start | bytes 294920 | tf_op jit(solution)/shard_map/ppermute | solution.py:25
  53.1 6.6 %collective-permute-start.2 = (bf16[128,384]{0,1:T(8,128)(2,1)S(1)}, bf16[128,384]{0,1:T(8,128)(2,1)S(1)}, u32[]{:S(2)}, u32[]{:S(2)}) collective-permute-start(bf16[128,384]{0,1:T(8,128)(2,1)S(1)} %collective-permute-done), channel_id=1, source_target_pairs={{0,1},{1,2},{2,3},{3,4},{4,5},{5,6},{6,7},{7,8},{8,9},{9,10},{10,1... | collective-permute-start | bytes 294920 | tf_op jit(solution)/shard_map/ppermute | solution.py:20
  55.1 6.6 %collective-permute-start.5 = (bf16[128,384]{0,1:T(8,128)(2,1)S(1)}, bf16[128,384]{0,1:T(8,128)(2,1)S(1)}, u32[]{:S(2)}, u32[]{:S(2)}) collective-permute-start(bf16[128,384]{0,1:T(8,128)(2,1)S(1)} %collective-permute-done.3), channel_id=1, source_target_pairs={{0,15},{1,0},{2,1},{3,2},{4,3},{5,4},{6,5},{7,6},{8,7},{9,8},{10,9... | collective-permute-start | bytes 294920 | tf_op jit(solution)/shard_map/ppermute | solution.py:25
  59.7 6.6 %collective-permute-start.4 = (bf16[128,384]{0,1:T(8,128)(2,1)S(1)}, bf16[128,384]{0,1:T(8,128)(2,1)S(1)}, u32[]{:S(2)}, u32[]{:S(2)}) collective-permute-start(bf16[128,384]{0,1:T(8,128)(2,1)S(1)} %collective-permute-done.2), channel_id=1, source_target_pairs={{0,1},{1,2},{2,3},{3,4},{4,5},{5,6},{6,7},{7,8},{8,9},{9,10},{10,1... | collective-permute-start | bytes 294920 | tf_op jit(solution)/shard_map/ppermute | solution.py:20
  61.7 6.6 %collective-permute-start.7 = (bf16[128,384]{0,1:T(8,128)(2,1)S(1)}, bf16[128,384]{0,1:T(8,128)(2,1)S(1)}, u32[]{:S(2)}, u32[]{:S(2)}) collective-permute-start(bf16[128,384]{0,1:T(8,128)(2,1)S(1)} %collective-permute-done.5), channel_id=1, source_target_pairs={{0,15},{1,0},{2,1},{3,2},{4,3},{5,4},{6,5},{7,6},{8,7},{9,8},{10,9... | collective-permute-start | bytes 294920 | tf_op jit(solution)/shard_map/ppermute | solution.py:25
  66.3 6.9 %collective-permute-start.6 = (bf16[128,384]{0,1:T(8,128)(2,1)S(1)}, bf16[128,384]{0,1:T(8,128)(2,1)S(1)}, u32[]{:S(2)}, u32[]{:S(2)}) collective-permute-start(bf16[128,384]{0,1:T(8,128)(2,1)S(1)} %collective-permute-done.4), channel_id=1, source_target_pairs={{0,1},{1,2},{2,3},{3,4},{4,5},{5,6},{6,7},{7,8},{8,9},{9,10},{10,1... | collective-permute-start | bytes 294920 | tf_op jit(solution)/shard_map/ppermute | solution.py:20
  68.3 7.1 %collective-permute-start.9 = (bf16[128,384]{0,1:T(8,128)(2,1)S(1)}, bf16[128,384]{0,1:T(8,128)(2,1)S(1)}, u32[]{:S(2)}, u32[]{:S(2)}) collective-permute-start(bf16[128,384]{0,1:T(8,128)(2,1)S(1)} %collective-permute-done.7), channel_id=1, source_target_pairs={{0,15},{1,0},{2,1},{3,2},{4,3},{5,4},{6,5},{7,6},{8,7},{9,8},{10,9... | collective-permute-start | bytes 294920 | tf_op jit(solution)/shard_map/ppermute | solution.py:25
  73.2 7.6 %collective-permute-start.8 = (bf16[128,384]{0,1:T(8,128)(2,1)S(1)}, bf16[128,384]{0,1:T(8,128)(2,1)S(1)}, u32[]{:S(2)}, u32[]{:S(2)}) collective-permute-start(bf16[128,384]{0,1:T(8,128)(2,1)S(1)} %collective-permute-done.6), channel_id=1, source_target_pairs={{0,1},{1,2},{2,3},{3,4},{4,5},{5,6},{6,7},{7,8},{8,9},{9,10},{10,1... | collective-permute-start | bytes 294920 | tf_op jit(solution)/shard_map/ppermute | solution.py:20
  75.4 7.4 %collective-permute-start.11 = (bf16[128,384]{0,1:T(8,128)(2,1)S(1)}, bf16[128,384]{0,1:T(8,128)(2,1)S(1)}, u32[]{:S(2)}, u32[]{:S(2)}) collective-permute-start(bf16[128,384]{0,1:T(8,128)(2,1)S(1)} %collective-permute-done.9), channel_id=1, source_target_pairs={{0,15},{1,0},{2,1},{3,2},{4,3},{5,4},{6,5},{7,6},{8,7},{9,8},{10,9... | collective-permute-start | bytes 294920 | tf_op jit(solution)/shard_map/ppermute | solution.py:25
  80.9 7.1 %collective-permute-start.10 = (bf16[128,384]{0,1:T(8,128)(2,1)S(1)}, bf16[128,384]{0,1:T(8,128)(2,1)S(1)}, u32[]{:S(2)}, u32[]{:S(2)}) collective-permute-start(bf16[128,384]{0,1:T(8,128)(2,1)S(1)} %collective-permute-done.8), channel_id=1, source_target_pairs={{0,1},{1,2},{2,3},{3,4},{4,5},{5,6},{6,7},{7,8},{8,9},{9,10},{10,1... | collective-permute-start | bytes 294920 | tf_op jit(solution)/shard_map/ppermute | solution.py:20
  82.8 13.6 %collective-permute-start.13 = (bf16[128,384]{0,1:T(8,128)(2,1)S(1)}, bf16[128,384]{0,1:T(8,128)(2,1)S(1)}, u32[]{:S(2)}, u32[]{:S(2)}) collective-permute-start(bf16[128,384]{0,1:T(8,128)(2,1)S(1)} %collective-permute-done.11), channel_id=1, source_target_pairs={{0,15},{1,0},{2,1},{3,2},{4,3},{5,4},{6,5},{7,6},{8,7},{9,8},{10,9... | collective-permute-start | bytes 294920 | tf_op jit(solution)/shard_map/ppermute | solution.py:25
  87.9 6.6 %collective-permute-start.12 = (bf16[128,384]{0,1:T(8,128)(2,1)S(1)}, bf16[128,384]{0,1:T(8,128)(2,1)S(1)}, u32[]{:S(2)}, u32[]{:S(2)}) collective-permute-start(bf16[128,384]{0,1:T(8,128)(2,1)S(1)} %collective-permute-done.10), channel_id=1, source_target_pairs={{0,1},{1,2},{2,3},{3,4},{4,5},{5,6},{6,7},{7,8},{8,9},{9,10},{10,1... | collective-permute-start | bytes 294920 | tf_op jit(solution)/shard_map/ppermute | solution.py:20
  94.5 6.6 %collective-permute-start.14 = (bf16[128,384]{0,1:T(8,128)(2,1)S(1)}, bf16[128,384]{0,1:T(8,128)(2,1)S(1)}, u32[]{:S(2)}, u32[]{:S(2)}) collective-permute-start(bf16[128,384]{0,1:T(8,128)(2,1)S(1)} %collective-permute-done.12), channel_id=1, source_target_pairs={{0,1},{1,2},{2,3},{3,4},{4,5},{5,6},{6,7},{7,8},{8,9},{9,10},{10,1... | collective-permute-start | bytes 294920 | tf_op jit(solution)/shard_map/ppermute | solution.py:20
  199.1 40.2 %copy-start = (bf16[128,48,64]{0,2,1:T(8,128)(2,1)S(1)}, bf16[128,48,64]{0,2,1:T(8,128)(2,1)}, u32[]{:S(2)}) copy-start(bf16[128,48,64]{0,2,1:T(8,128)(2,1)} %get-tuple-element.310) | copy-start | bytes 2359300
  232.8 8.8 %copy-start.2 = (bf16[128,128,64]{1,2,0:T(8,128)(2,1)S(1)}, bf16[128,128,64]{1,2,0:T(8,128)(2,1)}, u32[]{:S(2)}) copy-start(bf16[128,128,64]{1,2,0:T(8,128)(2,1)} %gather_fusion.2) | copy-start | bytes 6291460
  232.8 25.5 %collective-permute-start.17 = (bf16[8,8192]{1,0:T(8,128)(2,1)S(1)}, bf16[8,8192]{1,0:T(8,128)(2,1)S(1)}, u32[]{:S(2)}, u32[]{:S(2)}) collective-permute-start(bf16[8,8192]{1,0:T(8,128)(2,1)S(1)} %fusion), channel_id=1, source_target_pairs={{0,3},{1,4},{2,5},{3,6},{4,7},{5,8},{6,9},{7,10},{8,11},{9,12},{10... | collective-permute-start | bytes 393224
  234.3 24.1 %collective-permute-start.16 = (bf16[8,8192]{1,0:T(8,128)(2,1)S(1)}, bf16[8,8192]{1,0:T(8,128)(2,1)S(1)}, u32[]{:S(2)}, u32[]{:S(2)}) collective-permute-start(bf16[8,8192]{1,0:T(8,128)(2,1)S(1)} %fusion), channel_id=1, source_target_pairs={{0,2},{1,3},{2,4},{3,5},{4,6},{5,7},{6,8},{7,9},{8,10},{9,11},{10,... | collective-permute-start | bytes 393224
  236.9 21.5 %collective-permute-start.15 = (bf16[8,8192]{1,0:T(8,128)(2,1)S(1)}, bf16[8,8192]{1,0:T(8,128)(2,1)S(1)}, u32[]{:S(2)}, u32[]{:S(2)}) collective-permute-start(bf16[8,8192]{1,0:T(8,128)(2,1)S(1)} %fusion), channel_id=1, source_target_pairs={{0,1},{1,2},{2,3},{3,4},{4,5},{5,6},{6,7},{7,8},{8,9},{9,10},{10,1... | collective-permute-start | bytes 393224
  245.7 10.1 %copy-start.4 = (pred[128]{0:T(512)(128)(4,1)S(1)}, pred[128]{0:T(512)(128)(4,1)}, u32[]{:S(2)}) copy-start(pred[128]{0:T(512)(128)(4,1)} %iota_compare_fusion) | copy-start | bytes 388
  249.1 9.3 %collective-permute-start.18 = (bf16[6,8192]{1,0:T(8,128)(2,1)S(1)}, bf16[6,8192]{1,0:T(8,128)(2,1)S(1)}, u32[]{:S(2)}, u32[]{:S(2)}) collective-permute-start(bf16[6,8192]{1,0:T(8,128)(2,1)S(1)} %slice.8), channel_id=1, source_target_pairs={{0,4},{1,5},{2,6},{3,7},{4,8},{5,9},{6,10},{7,11},{8,12},{9,13},{1... | collective-permute-start | bytes 294920
  (4 other events, 27.7 us)
Sparse Core Ops, SparseCore 0:
  23.7 56.8 all-gather.1
  258.5 147.3 all-reduce.7
